TPU v7x, 32 devices: a whole 2x2x4 slice. The times are simulated.
32 devices in a mesh: gx: 8 (over z, x), gy: 4 (over y, core).
Axes of the slice: x: 2, y: 2, z: 4, core: 2. Of those that a mesh axis runs over, the one named last changes fastest.
Arguments:
- particles: float32 [4, 65536], P(None, ('gx', 'gy')), may hold values from -1 to 1, as said below
- tree_cells: float32 [10, 262144], P(None, ('gx', 'gy')), may hold values from -1 to 1, as said below
- let_list: int32 [32, 32, 4], P(('gx', 'gy')), may hold values from 0 to 63
- let_count: int32 [32, 32], P(('gx', 'gy')), may hold values from 1 to 4, as said below
- part_list: int32 [32, 4, 4], P(('gx', 'gy')), may hold values from 0 to 15
- cell_lists: int32 [512, 16], P(('gx', 'gy')), may hold values from 0 to 191
- near_lists: int32 [512, 8], P(('gx', 'gy')), may hold values from 0 to 31
Outputs:
- forces: float32 [4, 65536], P(None, ('gx', 'gy'))
Inputs may be any that keep to these rules, and one draw needn't show every extreme that they name: let_count is 4 wherever sender and receiver are at most 2 apart along gx+gy, and between 1 and 4 elsewhere. `particles`: positions lie in [-1, 1], masses are positive. `tree_cells`: centres lie in [-1, 1], masses are positive, the quadrupole is traceless.
All inputs are finite; a program needn't handle non-finite values.
Results may differ from a plain program's by a relative error of at most 0.0003.
Values sent between devices are 32-bit elements; how exact they have to be, the bound alone decides.
No kernel may reach another device: no remote copies, remote signals or barrier semaphores. Data moves between devices by JAX's collectives and lax.ppermute only.
A program may use at most 64 MiB of HBM per device.

v0:
```python
import functools

import jax
import jax.numpy as jnp
from jax import lax
from jax.experimental import pallas as pl
from jax.experimental.pallas import tpu as pltpu
from jax.sharding import PartitionSpec as P

BLK = 128
ROWS = 16
SUMS = 4
SOFTENING = 0.0025
near_offsets = (1, -1, 2, -2)
F32 = jnp.float32
B16 = jnp.bfloat16


def at_block(index):
    return pl.ds(pl.multiple_of(index * BLK, BLK), BLK)


def split3(value):
    high = value.astype(B16)
    rest = value - high.astype(F32)
    middle = rest.astype(B16)
    low = (rest - middle.astype(F32)).astype(B16)
    return high, middle, low


def split2(value):
    high = value.astype(B16)
    return high, (value - high.astype(F32)).astype(B16)


def stack_rows(rows):
    sub = lax.broadcasted_iota(jnp.int32, (8, BLK), 0)
    out = rows[0]
    for i in range(1, len(rows)):
        out = jnp.where(sub == i, rows[i], out)
    return out


def wide(row):
    return jnp.broadcast_to(row, (8, BLK))


def quadrupole_rows(x, y, z, xx, yy, xy, xz, yz):
    xx, yy, xy, xz, yz = (2.5 * v for v in (xx, yy, xy, xz, yz))
    zz = -(xx + yy)
    qx = xx * x + xy * y + xz * z
    qy = xy * x + yy * y + yz * z
    qz = xz * x + yz * y + zz * z
    inner = qx * x + qy * y + qz * z
    return [qx, qy, qz, inner, xx, yy, zz, xy, yz, xz]


def target_rows(x, y, z):
    one = jnp.ones((8, BLK), F32)
    first = stack_rows([-2 * x, -2 * y, -2 * z, one, x * x, y * y, z * z, 2 * x * y])
    second = stack_rows([2 * y * z, 2 * x * z] + [jnp.zeros((8, BLK), F32)] * 6)
    return jnp.concatenate([first, second], axis=0)


def six(weights):
    high, middle, low = weights[0:ROWS], weights[ROWS : 2 * ROWS], weights[2 * ROWS :]
    return jnp.concatenate([high, high, high, middle, middle, low], axis=0)


def contract(left, right):
    return lax.dot_general(left, right, (((1,), (1,)), ((), ())), preferred_element_type=F32)


def fetch(sources, targets, arrived):
    copies = [
        pltpu.make_async_copy(source, target, arrived.at[i])
        for i, (source, target) in enumerate(zip(sources, targets))
    ]
    for copy in copies:
        copy.start()
    for copy in copies:
        copy.wait()


def pick_kernel(*refs):
    chosen = refs[5]
    let_list, let_count, part_list, cells, particles, arrived = refs[6:]
    fetch(refs[:5], refs[6:11], arrived)
    slots, peers = let_list.shape
    sub = lax.broadcasted_iota(jnp.int32, (4, BLK), 0)

    def peer_step(d, unused):
        count = let_count[0, d]
        for k in range(slots):
            columns = at_block(let_list[k, d])
            live = k < count
            chosen[d, k] = jnp.where(live, cells[0:4, columns], 0.0)
            quad = jnp.where(sub == 2, cells[8:9, columns], cells[4:8, columns])
            chosen[d, slots + k] = jnp.where(live, quad, 0.0)
            chosen[d, 2 * slots, k : k + 1, :] = jnp.where(live, cells[9:10, columns], 0.0)
        return unused

    lax.fori_loop(0, peers, peer_step, 0, unroll=4)
    for position, offset in enumerate(near_offsets):
        d = lax.axis_index(("gx", "gy")) + offset

        @pl.when((d >= 0) & (d < peers))
        def _():
            for k in range(part_list.shape[1]):
                chosen[d, 2 * slots + 1 + k] = particles[:, at_block(part_list[position, k])]


def put_eight(first, fields, rows):
    for i, value in enumerate(fields):
        rows[pl.ds(first * ROWS + i, 8, stride=ROWS), :] = value
    for i in range(len(fields), ROWS):
        rows[pl.ds(first * ROWS + i, 8, stride=ROWS), :] = jnp.zeros((8, BLK), F32)


def put_weights(count, rows, weights):
    def step(b, unused):
        high, middle, low = split3(rows[pl.ds(pl.multiple_of(b * ROWS, ROWS), ROWS), :])
        weights[b, 0:ROWS] = high
        weights[b, ROWS : 2 * ROWS] = middle
        weights[b, 2 * ROWS :] = low
        return unused

    lax.fori_loop(0, count, step, 0, unroll=8)


def cell_group(size, j, first, lists, targets, spread, places, weights, sums, quads):
    blocks = [lists[j, first + i] for i in range(size)]
    coefficients = jnp.concatenate([six(weights[b]) for b in blocks], axis=1)
    bent = jnp.dot(targets[j], coefficients, preferred_element_type=F32)
    left = []
    for low in range(0, BLK, 16):
        rows = slice(low, low + 16)
        x, y, z = (spread[j, f, rows] for f in range(3))
        ax, ay, az, potential = (sums[j, f, rows] for f in range(SUMS))
        parts = []
        for i, b in enumerate(blocks):
            rx, ry, rz = x - places[b, 0:1, :], y - places[b, 1:2, :], z - places[b, 2:3, :]
            inverse = lax.rsqrt(rx * rx + ry * ry + (rz * rz + SOFTENING))
            square = inverse * inverse
            fifth = square * square * inverse
            pulled = inverse * places[b, 3:4, :]
            radial = square * (pulled + bent[rows, i * BLK : (i + 1) * BLK] * fifth)
            ax += radial * rx
            ay += radial * ry
            az += radial * rz
            potential += pulled
            parts += split2(fifth)
        for f, value in enumerate((ax, ay, az, potential)):
            sums[j, f, rows] = value
        left.append(jnp.concatenate(parts, axis=1))
    right = jnp.concatenate([weights[b] for b in blocks for _ in range(2)], axis=1)
    quads[j, :, : 3 * ROWS] += contract(jnp.concatenate(left, axis=0), right)


def near_group(size, j, first, lists, spread, places, sums):
    blocks = [lists[j, first + i] for i in range(size)]
    for low in range(0, BLK, 16):
        rows = slice(low, low + 16)
        x, y, z = (spread[j, f, rows] for f in range(3))
        ax, ay, az, potential = (sums[j, f, rows] for f in range(SUMS))
        for b in blocks:
            rx, ry, rz = x - places[b, 0:1, :], y - places[b, 1:2, :], z - places[b, 2:3, :]
            inverse = lax.rsqrt(rx * rx + ry * ry + (rz * rz + SOFTENING))
            pulled = inverse * places[b, 3:4, :]
            radial = pulled * (inverse * inverse)
            ax += radial * rx
            ay += radial * ry
            az += radial * rz
            potential += pulled
        for f, value in enumerate((ax, ay, az, potential)):
            sums[j, f, rows] = value


def in_groups(count, group):
    fours = (count + 1) // 4

    def four(i, unused):
        group(4, 4 * i)
        return unused

    lax.fori_loop(0, fours, four, 0)

    @pl.when(4 * fours < count)
    def _():
        group(2, 4 * fours)


def keep_some(j, source, width, base, target, counts, live, nothing):
    count = jnp.int32(0)
    for l in range(width):
        index = source(j, l)
        target[j, count] = index - base
        count = count + live(index)
    for extra in range(3):
        target[j, count + extra] = nothing
    counts[j] = count


def selectors():
    shape = (ROWS, (3 + 2 * SUMS) * BLK)
    row = lax.broadcasted_iota(jnp.int32, shape, 0)
    lane = lax.broadcasted_iota(jnp.int32, shape, 1)
    inside = lane % BLK
    quad = (lane < 3 * BLK) & (inside < 3 * ROWS) & (inside % ROWS == row) & (row < 10)
    total = (lane >= 3 * BLK) & ((lane - 3 * BLK) // (2 * BLK) == row - (ROWS - SUMS))
    return jnp.where(quad | total, 1.0, 0.0).astype(B16)


def forces_of(j, chooser, particles, sums, quads):
    parts = list(split3(quads[j]))
    for f in range(SUMS):
        parts += split2(sums[j, f])
    mixed = contract(chooser, jnp.concatenate(parts, axis=1))
    qx, qy, qz, inner, xx, yy, zz, xy, yz, xz = (mixed[i : i + 1] for i in range(10))
    sx, sy, sz, pulls = (mixed[ROWS - SUMS + f : ROWS - SUMS + f + 1] for f in range(SUMS))
    x, y, z = (particles[f : f + 1, at_block(j)] for f in range(3))
    ax = xx * x + xy * y + xz * z
    ay = xy * x + yy * y + yz * z
    az = xz * x + yz * y + zz * z
    bent = ax * x + ay * y + az * z - 2 * (qx * x + qy * y + qz * z) + inner
    return (
        0.4 * (ax - qx) - sx,
        0.4 * (ay - qy) - sy,
        0.4 * (az - qz) - sz,
        -pulls - 0.2 * bent,
    )


def own_kernel(*refs):
    out, targets_out = refs[4:6]
    (lists, list_counts, near_kept, near_counts, places, weights, near_places, fields, rows) = refs[6:15]
    targets, spread, sums, quads, sent, cell_lists, near_lists, particles, cells, arrived = refs[15:]
    fetch(refs[:4], refs[20:24], arrived)
    blocks = cell_lists.shape[0]
    own_cells = cells.shape[1] // BLK

    def by_field(b, unused):
        fields[pl.ds(b, 8, stride=own_cells), :] = cells[0:8, at_block(b)]
        fields[pl.ds(8 * own_cells + b, 2, stride=own_cells), :] = cells[8:10, at_block(b)]
        places[b] = cells[0:8, at_block(b)]
        return unused

    lax.fori_loop(0, own_cells, by_field, 0, unroll=8)

    def eight(g, unused):
        first = pl.multiple_of(8 * g, 8)
        x, y, z, _, xx, yy, _, xy, xz, yz = (
            fields[pl.ds(f * own_cells + first, 8), :] for f in range(10)
        )
        put_eight(first, quadrupole_rows(x, y, z, xx, yy, xy, xz, yz), rows)
        return unused

    lax.fori_loop(0, own_cells // 8, eight, 0, unroll=2)
    put_weights(own_cells, rows, weights)
    weights[own_cells] = jnp.zeros((3 * ROWS, BLK), B16)
    places[own_cells] = jnp.zeros((8, BLK), F32)
    near_places[blocks] = jnp.zeros((8, BLK), F32)

    lane = lax.broadcasted_iota(jnp.int32, (BLK, BLK), 1)
    unit = jnp.where(lax.broadcasted_iota(jnp.int32, (BLK, BLK), 0) == lane, 1.0, 0.0).astype(B16)
    pick = coordinates()

    def prepare_target(j, unused):
        near_places[j, 0:4, :] = particles[:, at_block(j)]
        x, y, z = (wide(particles[f : f + 1, at_block(j)]) for f in range(3))
        high, middle, low = split3(target_rows(x, y, z))
        turned = contract(unit, jnp.concatenate([high, middle, low, high, middle, high], axis=0))
        turned = turned.astype(B16)
        targets[j] = turned
        begin_block(j, turned, pick, spread, sums, quads)
        keep_some(
            j, lambda j, l: cell_lists[j, l], cell_lists.shape[1], 0, lists, list_counts,
            lambda b: (b < own_cells).astype(jnp.int32), own_cells,
        )
        keep_some(
            j, lambda j, l: near_lists[l, j], near_lists.shape[0], 0, near_kept, near_counts,
            lambda b: (b < blocks).astype(jnp.int32), blocks,
        )
        return unused

    lax.fori_loop(0, blocks, prepare_target, 0, unroll=4)
    hand_on = pltpu.make_async_copy(targets, targets_out, sent.at[0])
    hand_on.start()
    add_all(
        blocks, lists, list_counts, near_kept, near_counts, targets, spread, places, weights,
        near_places, sums, quads,
    )
    chooser = selectors()

    def finish_step(j, unused):
        for f, row in enumerate(forces_of(j, chooser, particles, sums, quads)):
            out[f : f + 1, at_block(j)] = row
        return unused

    lax.fori_loop(0, blocks, finish_step, 0, unroll=4)
    hand_on.wait()


def coordinates():
    shape = (6 * ROWS, 3 * BLK)
    row = lax.broadcasted_iota(jnp.int32, shape, 0)
    axis = lax.broadcasted_iota(jnp.int32, shape, 1) // BLK
    return jnp.where((row % ROWS == axis) & (row < 3 * ROWS), -0.5, 0.0).astype(B16)


def begin_block(j, turned, pick, spread, sums, quads):
    wider = jnp.dot(turned, pick, preferred_element_type=F32)
    for f in range(3):
        spread[j, f] = wider[:, f * BLK : (f + 1) * BLK]
    for f in range(SUMS):
        sums[j, f] = jnp.zeros((BLK, BLK), F32)
    quads[j] = jnp.zeros((BLK, BLK), F32)


def add_all(
    blocks, lists, list_counts, near_kept, near_counts, targets, spread, places, weights,
    near_places, sums, quads,
):
    def block_step(j, unused):
        in_groups(
            list_counts[j],
            lambda size, first: cell_group(
                size, j, first, lists, targets, spread, places, weights, sums, quads
            ),
        )
        in_groups(
            near_counts[j],
            lambda size, first: near_group(size, j, first, near_kept, spread, near_places, sums),
        )
        return unused

    lax.fori_loop(0, blocks, block_step, 0)


def moved_kernel(own_cells, near_slots, *refs):
    out = refs[6]
    (lists, list_counts, near_kept, near_counts, places, weights, near_places, fields, rows) = refs[7:16]
    spread, sums, quads, live = refs[16:20]
    cell_lists, near_lists, particles, targets, partial, moved, arrived = refs[20:]
    fetch(refs[:6], refs[20:26], arrived)
    blocks = cell_lists.shape[0]
    peers, slots = moved.shape[0], moved.shape[2]
    count = peers * slots
    near_moved = len(near_offsets) * near_slots
    me = lax.axis_index(("gx", "gy"))

    def by_field(s, unused):
        for k in range(slots):
            b = s * slots + k
            fields[pl.ds(b, 4, stride=count), :] = moved[s, k]
            fields[pl.ds(4 * count + b, 4, stride=count), :] = moved[s, slots + k]
            places[b, 0:4, :] = moved[s, k]
        fields[pl.ds(8 * count + s * slots, slots), :] = moved[s, 2 * slots]
        return unused

    lax.fori_loop(0, peers, by_field, 0, unroll=2)

    def none_live(b, unused):
        live[b] = 0
        return unused

    lax.fori_loop(0, own_cells, none_live, 0, unroll=8)
    bit = lax.broadcasted_iota(jnp.int32, (8, BLK), 0)

    def eight(g, unused):
        first = pl.multiple_of(8 * g, 8)
        x, y, z, mass, xx, yy, xz, xy, yz = (
            fields[pl.ds(f * count + first, 8), :] for f in range(9)
        )
        put_eight(first, quadrupole_rows(x, y, z, xx, yy, xy, xz, yz), rows)
        some = (mass != 0) | (xx != 0) | (yy != 0) | (xy != 0) | (xz != 0) | (yz != 0)
        some = jnp.max(jnp.where(some, 1.0, 0.0), axis=1, keepdims=True)
        code = jnp.sum(some * jnp.left_shift(1, bit[:, 0:1]).astype(F32)).astype(jnp.int32)
        for i in range(8):
            live[own_cells + first + i] = jnp.right_shift(code, i) & 1
        return unused

    lax.fori_loop(0, count // 8, eight, 0, unroll=4)
    put_weights(count, rows, weights)
    weights[count] = jnp.zeros((3 * ROWS, BLK), B16)
    places[count] = jnp.zeros((8, BLK), F32)
    for position, offset in enumerate(near_offsets):
        source = me - offset
        there = (source >= 0) & (source < peers)
        safe = jnp.clip(source, 0, peers - 1)
        for k in range(near_slots):
            block = moved[safe, 2 * slots + 1 + k]
            near_places[position * near_slots + k, 0:4, :] = jnp.where(there, block, 0.0)
    near_places[near_moved] = jnp.zeros((8, BLK), F32)

    pick = coordinates()

    def prepare_target(j, unused):
        begin_block(j, targets[j], pick, spread, sums, quads)
        keep_some(
            j, lambda j, l: cell_lists[j, l], cell_lists.shape[1], own_cells, lists, list_counts,
            lambda b: live[b], count,
        )
        keep_some(
            j, lambda j, l: near_lists[l, j], near_lists.shape[0], blocks, near_kept, near_counts,
            lambda b: (b >= blocks).astype(jnp.int32), near_moved,
        )
        return unused

    lax.fori_loop(0, blocks, prepare_target, 0, unroll=4)
    add_all(
        blocks, lists, list_counts, near_kept, near_counts, targets, spread, places, weights,
        near_places, sums, quads,
    )

    chooser = selectors()

    def finish_step(j, unused):
        for f, row in enumerate(forces_of(j, chooser, particles, sums, quads)):
            out[f : f + 1, at_block(j)] = row + partial[f : f + 1, at_block(j)]
        return unused

    lax.fori_loop(0, blocks, finish_step, 0, unroll=4)


def scratch(blocks, cells, near, list_width, near_width):
    return [
        pltpu.SMEM((blocks, list_width + 4), jnp.int32),
        pltpu.SMEM((blocks,), jnp.int32),
        pltpu.SMEM((blocks, near_width + 4), jnp.int32),
        pltpu.SMEM((blocks,), jnp.int32),
        pltpu.VMEM((cells + 1, 8, BLK), F32),
        pltpu.VMEM((cells + 1, 3 * ROWS, BLK), B16),
        pltpu.VMEM((near + 1, 8, BLK), F32),
        pltpu.VMEM((10 * cells, BLK), F32),
        pltpu.VMEM((ROWS * cells, BLK), F32),
    ]


def body(particles, tree_cells, let_list, let_count, part_list, cell_lists, near_lists):
    peers = lax.axis_size(("gx", "gy"))
    slots = let_list.shape[2]
    near_slots = part_list.shape[2]
    blocks, list_width = cell_lists.shape
    near_width = near_lists.shape[1]
    own_cells = tree_cells.shape[1] // BLK
    far = pl.BlockSpec(memory_space=pltpu.HBM)
    vmem = pl.BlockSpec(memory_space=pltpu.VMEM)
    params = pltpu.CompilerParams(vmem_limit_bytes=60 * 2**20)

    def landing(numbers, arrays):
        spaces = [pltpu.SMEM(a.shape, a.dtype) for a in numbers]
        spaces += [pltpu.VMEM(a.shape, a.dtype) for a in arrays]
        return spaces + [pltpu.SemaphoreType.DMA((len(spaces),))]

    choice = [jnp.transpose(let_list[0]), let_count, part_list[0]]
    chosen = pl.pallas_call(
        pick_kernel,
        out_shape=jax.ShapeDtypeStruct((peers, 2 * slots + 1 + near_slots, 4, BLK), F32),
        in_specs=[far] * 5,
        out_specs=vmem,
        scratch_shapes=landing(choice, [tree_cells, particles]),
        compiler_params=params,
    )(*choice, tree_cells, particles)
    moved = lax.all_to_all(chosen, ("gx", "gy"), split_axis=0, concat_axis=0, tiled=True)

    numbers = [cell_lists, jnp.transpose(near_lists)]
    targets = jax.ShapeDtypeStruct((blocks, BLK, 6 * ROWS), B16)
    sums = [
        pltpu.VMEM((blocks, 3, BLK, BLK), F32),
        pltpu.VMEM((blocks, SUMS, BLK, BLK), F32),
        pltpu.VMEM((blocks, BLK, BLK), F32),
    ]
    partial, turned = pl.pallas_call(
        own_kernel,
        out_shape=[jax.ShapeDtypeStruct(particles.shape, F32), targets],
        in_specs=[far] * 4,
        out_specs=[vmem, far],
        scratch_shapes=scratch(blocks, own_cells, blocks, list_width, near_width)
        + [pltpu.VMEM(targets.shape, targets.dtype)]
        + sums
        + [pltpu.SemaphoreType.DMA((1,))]
        + landing(numbers, [particles, tree_cells]),
        compiler_params=params,
        cost_estimate=pl.CostEstimate(flops=10**9, bytes_accessed=10**6, transcendentals=10**6),
    )(*numbers, particles, tree_cells)

    return pl.pallas_call(
        functools.partial(moved_kernel, own_cells, near_slots),
        out_shape=jax.ShapeDtypeStruct(particles.shape, F32),
        in_specs=[far] * 6,
        out_specs=vmem,
        scratch_shapes=scratch(
            blocks, peers * slots, len(near_offsets) * near_slots, list_width, near_width
        )
        + sums
        + [pltpu.SMEM((own_cells + peers * slots,), jnp.int32)]
        + landing(numbers, [particles, turned, partial, moved]),
        compiler_params=params,
    )(*numbers, particles, turned, partial, moved)


def solution(mesh):
    return jax.shard_map(
        body,
        mesh=mesh,
        in_specs=(
            P(None, ("gx", "gy")),
            P(None, ("gx", "gy")),
            P(("gx", "gy"), None, None),
            P(("gx", "gy"), None),
            P(("gx", "gy"), None, None),
            P(("gx", "gy"), None),
            P(("gx", "gy"), None),
        ),
        out_specs=P(None, ("gx", "gy")),
        check_vma=False,
    )
```

profile of v0, /device:TPU:3, one launch (start us, length us, event | category | flops | bytes accessed | tf_op | source)
XLA Modules:
  0.0 54.9 jit_solution(9701477916115875833)
XLA Ops:
  0.0 2.5 %shard_map.74 = f32[32,13,4,128]{3,2,1,0:T(4,128)} custom-call(s32[4,32]{1,0:T(4,128)} %bitcast.7, s32[1,32]{1,0:T(1,128)} %refs_1_.1, s32[4,4]{1,0:T(4,128)} %bitcast.8, f32[10,8192]{1,0:T(8,128)} %refs_3_.3, f32[4,2048]{1,0:T(4,128)} %refs_2_.3), custom_call_target="tpu_custom_call" | custom-call | tf_op jit(solution)/shard_map/pallas_call | solution.py:457
  2.5 6.4 %all-to-all-start = ((f32[32,13,4,128]{3,2,1,0:T(4,128)}), f32[32,13,4,128]{3,2,1,0:T(4,128)S(1)}, u32[]{:S(2)}, u32[]{:S(2)}) async-start(f32[32,13,4,128]{3,2,1,0:T(4,128)} %shard_map.74), calls=%async_computation | async-start | bytes 1703936 | tf_op jit(solution)/shard_map/all_to_all | solution.py:465
  9.0 18.9 %shard_map.73 = (f32[4,2048]{1,0:T(4,128)}, bf16[16,128,96]{2,1,0:T(8,128)(2,1)}) custom-call(s32[16,16]{1,0:T(8,128)} %refs_0_.3, s32[8,16]{1,0:T(8,128)} %bitcast.5, f32[4,2048]{1,0:T(4,128)} %refs_2_.3, f32[10,8192]{1,0:T(8,128)} %refs_3_.3), custom_call_target="tpu_custom_call" | custom-call | flops 1000000000 | bytes 1000000 | tf_op jit(solution)/shard_map/pallas_call | solution.py:474
  27.9 2.4 %all-to-all-done.refs_5_ = f32[32,13,4,128]{3,2,1,0:T(4,128)S(1)} async-done(((f32[32,13,4,128]{3,2,1,0:T(4,128)}), f32[32,13,4,128]{3,2,1,0:T(4,128)S(1)}, u32[]{:S(2)}, u32[]{:S(2)}) %all-to-all-start) | async-done | bytes 852000 | tf_op jit(solution)/shard_map/all_to_all | solution.py:465
  30.4 0.0 copy-start
  30.4 0.9 %copy-done = f32[32,13,4,128]{3,2,1,0:T(4,128)} copy-done((f32[32,13,4,128]{3,2,1,0:T(4,128)}, f32[32,13,4,128]{3,2,1,0:T(4,128)S(1)}, u32[]{:S(2)}) %copy-start) | copy-done | bytes 851992
  31.3 23.7 %shard_map.75 = f32[4,2048]{1,0:T(4,128)} custom-call(s32[16,16]{1,0:T(8,128)} %refs_0_.3, s32[8,16]{1,0:T(8,128)} %bitcast.6, f32[4,2048]{1,0:T(4,128)} %refs_2_.3, bf16[16,128,96]{2,1,0:T(8,128)(2,1)} %get-tuple-element.7.refs_3_, f32[4,2048]{1,0:T(4,128)} %get-tuple-element.8.refs_4_, f32[32,13,4,128]{3,2,1,0:T(4,128)} %copy-done), custom_call_target="tpu_custom_call" | custom-call | tf_op jit(solution)/shard_map/pallas_call | solution.py:488
Async XLA Ops:
  2.5 27.8 %all-to-all-start = ((f32[32,13,4,128]{3,2,1,0:T(4,128)}), f32[32,13,4,128]{3,2,1,0:T(4,128)S(1)}, u32[]{:S(2)}, u32[]{:S(2)}) async-start(f32[32,13,4,128]{3,2,1,0:T(4,128)} %shard_map.74), calls=%async_computation | async-start | bytes 1703936 | tf_op jit(solution)/shard_map/all_to_all | solution.py:465
  30.4 0.9 %copy-start = (f32[32,13,4,128]{3,2,1,0:T(4,128)}, f32[32,13,4,128]{3,2,1,0:T(4,128)S(1)}, u32[]{:S(2)}) copy-start(f32[32,13,4,128]{3,2,1,0:T(4,128)S(1)} %all-to-all-done.refs_5_) | copy-start | bytes 2555908
where the time goes:
time: 56 us; the launch traced here: 54.9 us
  Pallas kernels  45.1 us (81%)
  starting transfers between devices  6.44 us (12%)
  waiting for transfers between devices  2.44 us (4%)
  local copies, waits for them, and re-layouts  0.91 us (2%)
    pallas_call x1, Pallas kernels, body(): pl.pallas_call(functools.partial(moved_kernel, own_cells, near_slots), ou...  23.7 us
    pallas_call x1, Pallas kernels, body(): pl.pallas_call(own_kernel, out_shape=[jax.ShapeDtypeStruct(particles.shap...  18.9 us
    all_to_all x1, starting transfers between devices, body(): lax.all_to_all(chosen, ('gx', 'gy'), split_axis=0, concat_axis=0, tiled=T...  6.44 us
    pallas_call x1, Pallas kernels, body(): pl.pallas_call(pick_kernel, out_shape=jax.ShapeDtypeStruct((peers, 2 * sl...  2.54 us
    all_to_all x1, waiting for transfers between devices, body(): lax.all_to_all(chosen, ('gx', 'gy'), split_axis=0, concat_axis=0, tiled=T...  2.44 us
  transfers between devices with their start and end apart: 1, of which 1 were waited for; matrix products, arithmetic and copies ran while one was open for 0% of the time, Pallas kernels for 34%

commit v1 on v0

--- a/solution.py
+++ b/solution.py
@@ -78,6 +78,10 @@
     ]
     for copy in copies:
         copy.start()
+    return copies
+
+
+def wait_for(copies):
     for copy in copies:
         copy.wait()
 
@@ -85,7 +89,7 @@
 def pick_kernel(*refs):
     chosen = refs[5]
     let_list, let_count, part_list, cells, particles, arrived = refs[6:]
-    fetch(refs[:5], refs[6:11], arrived)
+    wait_for(fetch(refs[:5], refs[6:11], arrived))
     slots, peers = let_list.shape
     sub = lax.broadcasted_iota(jnp.int32, (4, BLK), 0)
 
@@ -128,66 +132,75 @@
     lax.fori_loop(0, count, step, 0, unroll=8)
 
 
-def cell_group(size, j, first, lists, targets, spread, places, weights, sums, quads):
-    blocks = [lists[j, first + i] for i in range(size)]
-    coefficients = jnp.concatenate([six(weights[b]) for b in blocks], axis=1)
-    bent = jnp.dot(targets[j], coefficients, preferred_element_type=F32)
+def group(cells, near, j, first, near_first, lists, near_kept, targets, spread, places, weights,
+          near_places, sums, quads):
+    blocks = [lists[j, first + i] for i in range(cells)]
+    near_blocks = [near_kept[j, near_first + i] for i in range(near)]
+    if cells:
+        coefficients = jnp.concatenate([six(weights[b]) for b in blocks], axis=1)
+        bent = jnp.dot(targets[j], coefficients, preferred_element_type=F32)
     left = []
     for low in range(0, BLK, 16):
         rows = slice(low, low + 16)
         x, y, z = (spread[j, f, rows] for f in range(3))
         ax, ay, az, potential = (sums[j, f, rows] for f in range(SUMS))
         parts = []
-        for i, b in enumerate(blocks):
-            rx, ry, rz = x - places[b, 0:1, :], y - places[b, 1:2, :], z - places[b, 2:3, :]
+        for i, (b, place) in enumerate(
+            [(b, near_places) for b in near_blocks] + [(b, places) for b in blocks]
+        ):
+            rx, ry, rz = x - place[b, 0:1, :], y - place[b, 1:2, :], z - place[b, 2:3, :]
             inverse = lax.rsqrt(rx * rx + ry * ry + (rz * rz + SOFTENING))
             square = inverse * inverse
-            fifth = square * square * inverse
-            pulled = inverse * places[b, 3:4, :]
-            radial = square * (pulled + bent[rows, i * BLK : (i + 1) * BLK] * fifth)
-            ax += radial * rx
-            ay += radial * ry
-            az += radial * rz
-            potential += pulled
-            parts += split2(fifth)
-        for f, value in enumerate((ax, ay, az, potential)):
-            sums[j, f, rows] = value
-        left.append(jnp.concatenate(parts, axis=1))
-    right = jnp.concatenate([weights[b] for b in blocks for _ in range(2)], axis=1)
-    quads[j, :, : 3 * ROWS] += contract(jnp.concatenate(left, axis=0), right)
-
-
-def near_group(size, j, first, lists, spread, places, sums):
-    blocks = [lists[j, first + i] for i in range(size)]
-    for low in range(0, BLK, 16):
-        rows = slice(low, low + 16)
-        x, y, z = (spread[j, f, rows] for f in range(3))
-        ax, ay, az, potential = (sums[j, f, rows] for f in range(SUMS))
-        for b in blocks:
-            rx, ry, rz = x - places[b, 0:1, :], y - places[b, 1:2, :], z - places[b, 2:3, :]
-            inverse = lax.rsqrt(rx * rx + ry * ry + (rz * rz + SOFTENING))
-            pulled = inverse * places[b, 3:4, :]
-            radial = pulled * (inverse * inverse)
+            pulled = inverse * place[b, 3:4, :]
+            if i < near:
+                radial = pulled * square
+            else:
+                fifth = square * square * inverse
+                columns = slice((i - near) * BLK, (i - near + 1) * BLK)
+                radial = square * (pulled + bent[rows, columns] * fifth)
+                parts += split2(fifth)
             ax += radial * rx
             ay += radial * ry
             az += radial * rz
             potential += pulled
         for f, value in enumerate((ax, ay, az, potential)):
             sums[j, f, rows] = value
-
-
-def in_groups(count, group):
-    fours = (count + 1) // 4
+        if cells:
+            left.append(jnp.concatenate(parts, axis=1))
+    if cells:
+        right = jnp.concatenate([weights[b] for b in blocks for _ in range(2)], axis=1)
+        quads[j, :, : 3 * ROWS] += contract(jnp.concatenate(left, axis=0), right)
+
+
+def add_block(j, count, near_count, *refs):
+    fours = jnp.where(count >= 6, (count - 2) // 4, 0)
+    fours = fours + (count - 4 * fours == 4).astype(jnp.int32)
+    rest = count - 4 * fours
 
     def four(i, unused):
-        group(4, 4 * i)
+        group(4, 0, j, 4 * i, 0, *refs)
         return unused
 
     lax.fori_loop(0, fours, four, 0)
-
-    @pl.when(4 * fours < count)
+    for size, beside in ((1, 2), (2, 2), (3, 2), (5, 0)):
+
+        @pl.when(rest == size)
+        def _():
+            group(size, beside, j, 4 * fours, 0, *refs)
+
+    done = jnp.where((rest >= 1) & (rest <= 3), 2, 0)
+    left = jnp.maximum(near_count - done, 0)
+    near_fours = (left + 1) // 4
+
+    def near_four(i, unused):
+        group(0, 4, j, 0, done + 4 * i, *refs)
+        return unused
+
+    lax.fori_loop(0, near_fours, near_four, 0)
+
+    @pl.when(4 * near_fours < left)
     def _():
-        group(2, 4 * fours)
+        group(0, 2, j, 0, done + 4 * near_fours, *refs)
 
 
 def keep_some(j, source, width, base, target, counts, live, nothing):
@@ -235,9 +248,11 @@
     out, targets_out = refs[4:6]
     (lists, list_counts, near_kept, near_counts, places, weights, near_places, fields, rows) = refs[6:15]
     targets, spread, sums, quads, sent, cell_lists, near_lists, particles, cells, arrived = refs[15:]
-    fetch(refs[:4], refs[20:24], arrived)
+    copies = fetch(refs[:4], refs[20:24], arrived)
     blocks = cell_lists.shape[0]
     own_cells = cells.shape[1] // BLK
+    clear(sums, quads)
+    wait_for(copies)
 
     def by_field(b, unused):
         fields[pl.ds(b, 8, stride=own_cells), :] = cells[0:8, at_block(b)]
@@ -272,7 +287,7 @@
         turned = contract(unit, jnp.concatenate([high, middle, low, high, middle, high], axis=0))
         turned = turned.astype(B16)
         targets[j] = turned
-        begin_block(j, turned, pick, spread, sums, quads)
+        begin_block(j, turned, pick, spread)
         keep_some(
             j, lambda j, l: cell_lists[j, l], cell_lists.shape[1], 0, lists, list_counts,
             lambda b: (b < own_cells).astype(jnp.int32), own_cells,
@@ -308,13 +323,20 @@
     return jnp.where((row % ROWS == axis) & (row < 3 * ROWS), -0.5, 0.0).astype(B16)
 
 
-def begin_block(j, turned, pick, spread, sums, quads):
+def begin_block(j, turned, pick, spread):
     wider = jnp.dot(turned, pick, preferred_element_type=F32)
     for f in range(3):
         spread[j, f] = wider[:, f * BLK : (f + 1) * BLK]
-    for f in range(SUMS):
-        sums[j, f] = jnp.zeros((BLK, BLK), F32)
-    quads[j] = jnp.zeros((BLK, BLK), F32)
+
+
+def clear(sums, quads):
+    def step(j, unused):
+        for f in range(SUMS):
+            sums[j, f] = jnp.zeros((BLK, BLK), F32)
+        quads[j] = jnp.zeros((BLK, BLK), F32)
+        return unused
+
+    lax.fori_loop(0, quads.shape[0], step, 0)
 
 
 def add_all(
@@ -322,15 +344,9 @@
     near_places, sums, quads,
 ):
     def block_step(j, unused):
-        in_groups(
-            list_counts[j],
-            lambda size, first: cell_group(
-                size, j, first, lists, targets, spread, places, weights, sums, quads
-            ),
-        )
-        in_groups(
-            near_counts[j],
-            lambda size, first: near_group(size, j, first, near_kept, spread, near_places, sums),
+        add_block(
+            j, list_counts[j], near_counts[j], lists, near_kept, targets, spread, places, weights,
+            near_places, sums, quads,
         )
         return unused
 
@@ -342,12 +358,20 @@
     (lists, list_counts, near_kept, near_counts, places, weights, near_places, fields, rows) = refs[7:16]
     spread, sums, quads, live = refs[16:20]
     cell_lists, near_lists, particles, targets, partial, moved, arrived = refs[20:]
-    fetch(refs[:6], refs[20:26], arrived)
+    copies = fetch(refs[:6], refs[20:26], arrived)
     blocks = cell_lists.shape[0]
     peers, slots = moved.shape[0], moved.shape[2]
     count = peers * slots
     near_moved = len(near_offsets) * near_slots
     me = lax.axis_index(("gx", "gy"))
+    clear(sums, quads)
+
+    def none_live(b, unused):
+        live[b] = 0
+        return unused
+
+    lax.fori_loop(0, own_cells, none_live, 0, unroll=8)
+    wait_for(copies)
 
     def by_field(s, unused):
         for k in range(slots):
@@ -358,13 +382,8 @@
         fields[pl.ds(8 * count + s * slots, slots), :] = moved[s, 2 * slots]
         return unused
 
-    lax.fori_loop(0, peers, by_field, 0, unroll=2)
-
-    def none_live(b, unused):
-        live[b] = 0
-        return unused
-
-    lax.fori_loop(0, own_cells, none_live, 0, unroll=8)
+    lax.fori_loop(0, peers, by_field, 0, unroll=4)
+
     bit = lax.broadcasted_iota(jnp.int32, (8, BLK), 0)
 
     def eight(g, unused):
@@ -380,7 +399,7 @@
             live[own_cells + first + i] = jnp.right_shift(code, i) & 1
         return unused
 
-    lax.fori_loop(0, count // 8, eight, 0, unroll=4)
+    lax.fori_loop(0, count // 8, eight, 0, unroll=8)
     put_weights(count, rows, weights)
     weights[count] = jnp.zeros((3 * ROWS, BLK), B16)
     places[count] = jnp.zeros((8, BLK), F32)
@@ -396,7 +415,7 @@
     pick = coordinates()
 
     def prepare_target(j, unused):
-        begin_block(j, targets[j], pick, spread, sums, quads)
+        begin_block(j, targets[j], pick, spread)
         keep_some(
             j, lambda j, l: cell_lists[j, l], cell_lists.shape[1], own_cells, lists, list_counts,
             lambda b: live[b], count,
@@ -481,7 +500,7 @@
         + sums
         + [pltpu.SemaphoreType.DMA((1,))]
         + landing(numbers, [particles, tree_cells]),
-        compiler_params=params,
+        compiler_params=pltpu.CompilerParams(vmem_limit_bytes=127 * 2**19),
         cost_estimate=pl.CostEstimate(flops=10**9, bytes_accessed=10**6, transcendentals=10**6),
     )(*numbers, particles, tree_cells)
 

time: 56 us -> 53.3 us (0.952)
  the two profiles are of different devices: /device:TPU:3 before, /device:TPU:0 now
where the time goes in v1:
time: 53.3 us; the launch traced here: 52.9 us
  Pallas kernels  42.8 us (80%)
  starting transfers between devices  7.42 us (14%)
  waiting for transfers between devices  2.63 us (5%)
    pallas_call x1, Pallas kernels, body(): pl.pallas_call(functools.partial(moved_kernel, own_cells, near_slots), ou...  20.9 us
    pallas_call x1, Pallas kernels, body(): pl.pallas_call(own_kernel, out_shape=[jax.ShapeDtypeStruct(particles.shap...  19.4 us
    all_to_all x1, starting transfers between devices, body(): lax.all_to_all(chosen, ('gx', 'gy'), split_axis=0, concat_axis=0, tiled=T...  7.42 us
    all_to_all x1, waiting for transfers between devices, body(): lax.all_to_all(chosen, ('gx', 'gy'), split_axis=0, concat_axis=0, tiled=T...  2.63 us
    pallas_call x1, Pallas kernels, body(): pl.pallas_call(pick_kernel, out_shape=jax.ShapeDtypeStruct((peers, 2 * sl...  2.56 us
  transfers between devices with their start and end apart: 1, of which 1 were waited for; matrix products, arithmetic and copies ran while one was open for 0% of the time, Pallas kernels for 37%

profile of v1, /device:TPU:0, one launch (start us, length us, event | category | flops | bytes accessed | tf_op | source)
XLA Modules:
  0.0 52.9 jit_solution(1690690113405048429)
XLA Ops:
  0.0 2.6 %shard_map.74 = f32[32,13,4,128]{3,2,1,0:T(4,128)} custom-call(s32[4,32]{1,0:T(4,128)} %bitcast.7, s32[1,32]{1,0:T(1,128)} %refs_1_.1, s32[4,4]{1,0:T(4,128)} %bitcast.8, f32[10,8192]{1,0:T(8,128)} %refs_3_.3, f32[4,2048]{1,0:T(4,128)} %refs_2_.3), custom_call_target="tpu_custom_call" | custom-call | tf_op jit(solution)/shard_map/pallas_call | solution.py:476
  2.6 7.4 %all-to-all-start = ((f32[32,13,4,128]{3,2,1,0:T(4,128)}), f32[32,13,4,128]{3,2,1,0:T(4,128)}, u32[]{:S(2)}, u32[]{:S(2)}) async-start(f32[32,13,4,128]{3,2,1,0:T(4,128)} %shard_map.74), calls=%async_computation | async-start | bytes 1703936 | tf_op jit(solution)/shard_map/all_to_all | solution.py:484
  10.0 19.4 %shard_map.73 = (f32[4,2048]{1,0:T(4,128)}, bf16[16,128,96]{2,1,0:T(8,128)(2,1)}) custom-call(s32[16,16]{1,0:T(8,128)} %refs_0_.3, s32[8,16]{1,0:T(8,128)} %bitcast.5, f32[4,2048]{1,0:T(4,128)} %refs_2_.3, f32[10,8192]{1,0:T(8,128)} %refs_3_.3), custom_call_target="tpu_custom_call" | custom-call | flops 1000000000 | bytes 1000000 | tf_op jit(solution)/shard_map/pallas_call | solution.py:493
  29.4 2.6 %all-to-all-done.refs_5_ = f32[32,13,4,128]{3,2,1,0:T(4,128)} async-done(((f32[32,13,4,128]{3,2,1,0:T(4,128)}), f32[32,13,4,128]{3,2,1,0:T(4,128)}, u32[]{:S(2)}, u32[]{:S(2)}) %all-to-all-start) | async-done | bytes 852000 | tf_op jit(solution)/shard_map/all_to_all | solution.py:484
  32.0 20.9 %shard_map.75 = f32[4,2048]{1,0:T(4,128)} custom-call(s32[16,16]{1,0:T(8,128)} %refs_0_.3, s32[8,16]{1,0:T(8,128)} %bitcast.6, f32[4,2048]{1,0:T(4,128)} %refs_2_.3, bf16[16,128,96]{2,1,0:T(8,128)(2,1)} %get-tuple-element.7.refs_3_, f32[4,2048]{1,0:T(4,128)} %get-tuple-element.8.refs_4_, f32[32,13,4,128]{3,2,1,0:T(4,128)} %all-to-all-done.refs_5_), custom_call_target="tpu_custom_call" | custom-call | tf_op jit(solution)/shard_map/pallas_call | solution.py:507
Async XLA Ops:
  2.6 29.4 %all-to-all-start = ((f32[32,13,4,128]{3,2,1,0:T(4,128)}), f32[32,13,4,128]{3,2,1,0:T(4,128)}, u32[]{:S(2)}, u32[]{:S(2)}) async-start(f32[32,13,4,128]{3,2,1,0:T(4,128)} %shard_map.74), calls=%async_computation | async-start | bytes 1703936 | tf_op jit(solution)/shard_map/all_to_all | solution.py:484

commit v2 on v1

--- a/solution.py
+++ b/solution.py
@@ -87,9 +87,9 @@
 
 
 def pick_kernel(*refs):
-    chosen = refs[5]
-    let_list, let_count, part_list, cells, particles, arrived = refs[6:]
-    wait_for(fetch(refs[:5], refs[6:11], arrived))
+    chosen_out = refs[5]
+    chosen, sent, let_list, let_count, part_list, cells, particles, arrived = refs[6:]
+    wait_for(fetch(refs[:5], refs[8:13], arrived))
     slots, peers = let_list.shape
     sub = lax.broadcasted_iota(jnp.int32, (4, BLK), 0)
 
@@ -104,7 +104,6 @@
             chosen[d, 2 * slots, k : k + 1, :] = jnp.where(live, cells[9:10, columns], 0.0)
         return unused
 
-    lax.fori_loop(0, peers, peer_step, 0, unroll=4)
     for position, offset in enumerate(near_offsets):
         d = lax.axis_index(("gx", "gy")) + offset
 
@@ -112,6 +111,15 @@
         def _():
             for k in range(part_list.shape[1]):
                 chosen[d, 2 * slots + 1 + k] = particles[:, at_block(part_list[position, k])]
+
+    chunks = sent.shape[0]
+    copies = []
+    for c in range(chunks):
+        part = slice(c * peers // chunks, (c + 1) * peers // chunks)
+        lax.fori_loop(part.start, part.stop, peer_step, 0, unroll=4)
+        copies.append(pltpu.make_async_copy(chosen.at[part], chosen_out.at[part], sent.at[c]))
+        copies[-1].start()
+    wait_for(copies)
 
 
 def put_eight(first, fields, rows):
@@ -121,15 +129,11 @@
         rows[pl.ds(first * ROWS + i, 8, stride=ROWS), :] = jnp.zeros((8, BLK), F32)
 
 
-def put_weights(count, rows, weights):
-    def step(b, unused):
-        high, middle, low = split3(rows[pl.ds(pl.multiple_of(b * ROWS, ROWS), ROWS), :])
-        weights[b, 0:ROWS] = high
-        weights[b, ROWS : 2 * ROWS] = middle
-        weights[b, 2 * ROWS :] = low
-        return unused
-
-    lax.fori_loop(0, count, step, 0, unroll=8)
+def put_weights(b, rows, weights):
+    high, middle, low = split3(rows[pl.ds(pl.multiple_of(b * ROWS, ROWS), ROWS), :])
+    weights[b, 0:ROWS] = high
+    weights[b, ROWS : 2 * ROWS] = middle
+    weights[b, 2 * ROWS :] = low
 
 
 def group(cells, near, j, first, near_first, lists, near_kept, targets, spread, places, weights,
@@ -172,7 +176,7 @@
         quads[j, :, : 3 * ROWS] += contract(jnp.concatenate(left, axis=0), right)
 
 
-def add_block(j, count, near_count, *refs):
+def add_block(j, count, near_count, list_next, *refs):
     fours = jnp.where(count >= 6, (count - 2) // 4, 0)
     fours = fours + (count - 4 * fours == 4).astype(jnp.int32)
     rest = count - 4 * fours
@@ -187,7 +191,9 @@
         @pl.when(rest == size)
         def _():
             group(size, beside, j, 4 * fours, 0, *refs)
-
+            list_next()
+
+    pl.when(rest == 0)(list_next)
     done = jnp.where((rest >= 1) & (rest <= 3), 2, 0)
     left = jnp.maximum(near_count - done, 0)
     near_fours = (left + 1) // 4
@@ -215,19 +221,25 @@
 
 
 def selectors():
-    shape = (ROWS, (3 + 2 * SUMS) * BLK)
+    shape = (ROWS, 7 * BLK)
     row = lax.broadcasted_iota(jnp.int32, shape, 0)
     lane = lax.broadcasted_iota(jnp.int32, shape, 1)
     inside = lane % BLK
     quad = (lane < 3 * BLK) & (inside < 3 * ROWS) & (inside % ROWS == row) & (row < 10)
-    total = (lane >= 3 * BLK) & ((lane - 3 * BLK) // (2 * BLK) == row - (ROWS - SUMS))
+    half = 2 * ((lane - 3 * BLK) // (2 * BLK)) + (inside >= BLK // 2).astype(jnp.int32)
+    total = (lane >= 3 * BLK) & (half == row - (ROWS - SUMS))
     return jnp.where(quad | total, 1.0, 0.0).astype(B16)
+
+
+def fold(first, second):
+    low = lax.broadcasted_iota(jnp.int32, first.shape, 1) < BLK // 2
+    return jnp.where(low, first, second) + pltpu.roll(jnp.where(low, second, first), BLK // 2, 1)
 
 
 def forces_of(j, chooser, particles, sums, quads):
     parts = list(split3(quads[j]))
-    for f in range(SUMS):
-        parts += split2(sums[j, f])
+    for f in range(0, SUMS, 2):
+        parts += split2(fold(sums[j, f], sums[j, f + 1]))
     mixed = contract(chooser, jnp.concatenate(parts, axis=1))
     qx, qy, qz, inner, xx, yy, zz, xy, yz, xz = (mixed[i : i + 1] for i in range(10))
     sx, sy, sz, pulls = (mixed[ROWS - SUMS + f : ROWS - SUMS + f + 1] for f in range(SUMS))
@@ -245,10 +257,10 @@
 
 
 def own_kernel(*refs):
-    out, targets_out = refs[4:6]
-    (lists, list_counts, near_kept, near_counts, places, weights, near_places, fields, rows) = refs[6:15]
-    targets, spread, sums, quads, sent, cell_lists, near_lists, particles, cells, arrived = refs[15:]
-    copies = fetch(refs[:4], refs[20:24], arrived)
+    out, targets_out, spread_out = refs[4:7]
+    (lists, list_counts, near_kept, near_counts, places, weights, near_places, fields, rows) = refs[7:16]
+    targets, spread, sums, quads, sent, cell_lists, near_lists, particles, cells, arrived = refs[16:]
+    copies = fetch(refs[:4], refs[21:25], arrived)
     blocks = cell_lists.shape[0]
     own_cells = cells.shape[1] // BLK
     clear(sums, quads)
@@ -271,7 +283,12 @@
         return unused
 
     lax.fori_loop(0, own_cells // 8, eight, 0, unroll=2)
-    put_weights(own_cells, rows, weights)
+
+    def step(b, unused):
+        put_weights(b, rows, weights)
+        return unused
+
+    lax.fori_loop(0, own_cells, step, 0, unroll=8)
     weights[own_cells] = jnp.zeros((3 * ROWS, BLK), B16)
     places[own_cells] = jnp.zeros((8, BLK), F32)
     near_places[blocks] = jnp.zeros((8, BLK), F32)
@@ -288,6 +305,11 @@
         turned = turned.astype(B16)
         targets[j] = turned
         begin_block(j, turned, pick, spread)
+        return unused
+
+    lax.fori_loop(0, blocks, prepare_target, 0, unroll=4)
+
+    def make_lists(j):
         keep_some(
             j, lambda j, l: cell_lists[j, l], cell_lists.shape[1], 0, lists, list_counts,
             lambda b: (b < own_cells).astype(jnp.int32), own_cells,
@@ -296,13 +318,10 @@
             j, lambda j, l: near_lists[l, j], near_lists.shape[0], 0, near_kept, near_counts,
             lambda b: (b < blocks).astype(jnp.int32), blocks,
         )
-        return unused
-
-    lax.fori_loop(0, blocks, prepare_target, 0, unroll=4)
-    hand_on = pltpu.make_async_copy(targets, targets_out, sent.at[0])
-    hand_on.start()
+
+    hand_on = fetch([targets, spread], [targets_out, spread_out], sent)
     add_all(
-        blocks, lists, list_counts, near_kept, near_counts, targets, spread, places, weights,
+        blocks, make_lists, lists, list_counts, near_kept, near_counts, targets, spread, places, weights,
         near_places, sums, quads,
     )
     chooser = selectors()
@@ -313,7 +332,7 @@
         return unused
 
     lax.fori_loop(0, blocks, finish_step, 0, unroll=4)
-    hand_on.wait()
+    wait_for(hand_on)
 
 
 def coordinates():
@@ -340,13 +359,15 @@
 
 
 def add_all(
-    blocks, lists, list_counts, near_kept, near_counts, targets, spread, places, weights,
+    blocks, make_lists, lists, list_counts, near_kept, near_counts, targets, spread, places, weights,
     near_places, sums, quads,
 ):
+    make_lists(0)
+
     def block_step(j, unused):
         add_block(
-            j, list_counts[j], near_counts[j], lists, near_kept, targets, spread, places, weights,
-            near_places, sums, quads,
+            j, list_counts[j], near_counts[j], lambda: make_lists(jnp.minimum(j + 1, blocks - 1)),
+            lists, near_kept, targets, spread, places, weights, near_places, sums, quads,
         )
         return unused
 
@@ -354,11 +375,11 @@
 
 
 def moved_kernel(own_cells, near_slots, *refs):
-    out = refs[6]
-    (lists, list_counts, near_kept, near_counts, places, weights, near_places, fields, rows) = refs[7:16]
-    spread, sums, quads, live = refs[16:20]
-    cell_lists, near_lists, particles, targets, partial, moved, arrived = refs[20:]
-    copies = fetch(refs[:6], refs[20:26], arrived)
+    out = refs[7]
+    (lists, list_counts, near_kept, near_counts, places, weights, near_places, fields, rows) = refs[8:17]
+    sums, quads, live = refs[17:20]
+    cell_lists, near_lists, moved, particles, targets, spread, partial, arrived = refs[20:]
+    copies = fetch(refs[:7], refs[20:27], arrived)
     blocks = cell_lists.shape[0]
     peers, slots = moved.shape[0], moved.shape[2]
     count = peers * slots
@@ -371,7 +392,7 @@
         return unused
 
     lax.fori_loop(0, own_cells, none_live, 0, unroll=8)
-    wait_for(copies)
+    wait_for(copies[:3])
 
     def by_field(s, unused):
         for k in range(slots):
@@ -400,7 +421,6 @@
         return unused
 
     lax.fori_loop(0, count // 8, eight, 0, unroll=8)
-    put_weights(count, rows, weights)
     weights[count] = jnp.zeros((3 * ROWS, BLK), B16)
     places[count] = jnp.zeros((8, BLK), F32)
     for position, offset in enumerate(near_offsets):
@@ -412,10 +432,13 @@
             near_places[position * near_slots + k, 0:4, :] = jnp.where(there, block, 0.0)
     near_places[near_moved] = jnp.zeros((8, BLK), F32)
 
-    pick = coordinates()
-
-    def prepare_target(j, unused):
-        begin_block(j, targets[j], pick, spread)
+    def step(b, unused):
+        put_weights(b, rows, weights)
+        return unused
+
+    lax.fori_loop(0, count, step, 0, unroll=8)
+
+    def make_lists(j):
         keep_some(
             j, lambda j, l: cell_lists[j, l], cell_lists.shape[1], own_cells, lists, list_counts,
             lambda b: live[b], count,
@@ -424,11 +447,10 @@
             j, lambda j, l: near_lists[l, j], near_lists.shape[0], blocks, near_kept, near_counts,
             lambda b: (b >= blocks).astype(jnp.int32), near_moved,
         )
-        return unused
-
-    lax.fori_loop(0, blocks, prepare_target, 0, unroll=4)
+
+    wait_for(copies[3:])
     add_all(
-        blocks, lists, list_counts, near_kept, near_counts, targets, spread, places, weights,
+        blocks, make_lists, lists, list_counts, near_kept, near_counts, targets, spread, places, weights,
         near_places, sums, quads,
     )
 
@@ -477,28 +499,31 @@
         pick_kernel,
         out_shape=jax.ShapeDtypeStruct((peers, 2 * slots + 1 + near_slots, 4, BLK), F32),
         in_specs=[far] * 5,
-        out_specs=vmem,
-        scratch_shapes=landing(choice, [tree_cells, particles]),
+        out_specs=far,
+        scratch_shapes=[
+            pltpu.VMEM((peers, 2 * slots + 1 + near_slots, 4, BLK), F32),
+            pltpu.SemaphoreType.DMA((4,)),
+        ]
+        + landing(choice, [tree_cells, particles]),
         compiler_params=params,
     )(*choice, tree_cells, particles)
     moved = lax.all_to_all(chosen, ("gx", "gy"), split_axis=0, concat_axis=0, tiled=True)
 
     numbers = [cell_lists, jnp.transpose(near_lists)]
-    targets = jax.ShapeDtypeStruct((blocks, BLK, 6 * ROWS), B16)
-    sums = [
-        pltpu.VMEM((blocks, 3, BLK, BLK), F32),
-        pltpu.VMEM((blocks, SUMS, BLK, BLK), F32),
-        pltpu.VMEM((blocks, BLK, BLK), F32),
+    turned = [
+        jax.ShapeDtypeStruct((blocks, BLK, 6 * ROWS), B16),
+        jax.ShapeDtypeStruct((blocks, 3, BLK, BLK), F32),
     ]
-    partial, turned = pl.pallas_call(
+    sums = [pltpu.VMEM((blocks, SUMS, BLK, BLK), F32), pltpu.VMEM((blocks, BLK, BLK), F32)]
+    partial, *turned = pl.pallas_call(
         own_kernel,
-        out_shape=[jax.ShapeDtypeStruct(particles.shape, F32), targets],
+        out_shape=[jax.ShapeDtypeStruct(particles.shape, F32)] + turned,
         in_specs=[far] * 4,
-        out_specs=[vmem, far],
+        out_specs=[vmem, far, far],
         scratch_shapes=scratch(blocks, own_cells, blocks, list_width, near_width)
-        + [pltpu.VMEM(targets.shape, targets.dtype)]
+        + [pltpu.VMEM(leaf.shape, leaf.dtype) for leaf in turned]
         + sums
-        + [pltpu.SemaphoreType.DMA((1,))]
+        + [pltpu.SemaphoreType.DMA((2,))]
         + landing(numbers, [particles, tree_cells]),
         compiler_params=pltpu.CompilerParams(vmem_limit_bytes=127 * 2**19),
         cost_estimate=pl.CostEstimate(flops=10**9, bytes_accessed=10**6, transcendentals=10**6),
@@ -507,16 +532,16 @@
     return pl.pallas_call(
         functools.partial(moved_kernel, own_cells, near_slots),
         out_shape=jax.ShapeDtypeStruct(particles.shape, F32),
-        in_specs=[far] * 6,
+        in_specs=[far] * 7,
         out_specs=vmem,
         scratch_shapes=scratch(
             blocks, peers * slots, len(near_offsets) * near_slots, list_width, near_width
         )
         + sums
         + [pltpu.SMEM((own_cells + peers * slots,), jnp.int32)]
-        + landing(numbers, [particles, turned, partial, moved]),
+        + landing(numbers, [moved, particles, *turned, partial]),
         compiler_params=params,
-    )(*numbers, particles, turned, partial, moved)
+    )(*numbers, moved, particles, *turned, partial)
 
 
 def solution(mesh):

time: 53.3 us -> 51.6 us (0.968)
  Pallas kernels: 42.8 us -> 40.5 us
    pallas_call x1, Pallas kernels: 20.9 us -> 19.3 us  [body(): pl.pallas_call(functools.partial(moved_kernel, own_cells, near_slots), ou...]
where the time goes in v2:
time: 51.6 us; the launch traced here: 51.1 us
  Pallas kernels  40.5 us (78%)
  starting transfers between devices  7.42 us (14%)
  waiting for transfers between devices  3.13 us (6%)
    pallas_call x1, Pallas kernels, body(): pl.pallas_call(functools.partial(moved_kernel, own_cells, near_slots), ou...  19.3 us
    pallas_call x1, Pallas kernels, body(): pl.pallas_call(own_kernel, out_shape=[jax.ShapeDtypeStruct(particles.shap...  18.9 us
    all_to_all x1, starting transfers between devices, body(): lax.all_to_all(chosen, ('gx', 'gy'), split_axis=0, concat_axis=0, tiled=T...  7.42 us
    all_to_all x1, waiting for transfers between devices, body(): lax.all_to_all(chosen, ('gx', 'gy'), split_axis=0, concat_axis=0, tiled=T...  3.13 us
    pallas_call x1, Pallas kernels, body(): pl.pallas_call(pick_kernel, out_shape=jax.ShapeDtypeStruct((peers, 2 * sl...  2.31 us
  transfers between devices with their start and end apart: 1, of which 1 were waited for; matrix products, arithmetic and copies ran while one was open for 0% of the time, Pallas kernels for 37%

profile of v2, /device:TPU:0, one launch (start us, length us, event | category | flops | bytes accessed | tf_op | source)
XLA Modules:
  0.0 51.1 jit_solution(3502658592243600540)
XLA Ops:
  0.0 2.3 %shard_map.73 = f32[32,13,4,128]{3,2,1,0:T(4,128)} custom-call(s32[4,32]{1,0:T(4,128)} %bitcast.7, s32[1,32]{1,0:T(1,128)} %refs_1_.1, s32[4,4]{1,0:T(4,128)} %bitcast.8, f32[10,8192]{1,0:T(8,128)} %refs_3_.4, f32[4,2048]{1,0:T(4,128)} %refs_3_.5), custom_call_target="tpu_custom_call" | custom-call | tf_op jit(solution)/shard_map/pallas_call | solution.py:498
  2.3 7.4 %all-to-all-start = ((f32[32,13,4,128]{3,2,1,0:T(4,128)}), f32[32,13,4,128]{3,2,1,0:T(4,128)}, u32[]{:S(2)}, u32[]{:S(2)}) async-start(f32[32,13,4,128]{3,2,1,0:T(4,128)} %shard_map.73), calls=%async_computation | async-start | bytes 1703936 | tf_op jit(solution)/shard_map/all_to_all | solution.py:510
  9.8 18.9 %shard_map.74 = (f32[4,2048]{1,0:T(4,128)}, bf16[16,128,96]{2,1,0:T(8,128)(2,1)}, f32[16,3,128,128]{3,2,1,0:T(8,128)}) custom-call(s32[16,16]{1,0:T(8,128)} %refs_0_.3, s32[8,16]{1,0:T(8,128)} %bitcast.5, f32[4,2048]{1,0:T(4,128)} %refs_3_.5, f32[10,8192]{1,0:T(8,128)} %refs_3_.4), custom_call_target="tpu_custom_call" | custom-call | flops 1000000000 | bytes 1000000 | tf_op jit(solution)/shard_map/pallas_call | solution.py:518
  28.6 3.1 %all-to-all-done.refs_2_ = f32[32,13,4,128]{3,2,1,0:T(4,128)} async-done(((f32[32,13,4,128]{3,2,1,0:T(4,128)}), f32[32,13,4,128]{3,2,1,0:T(4,128)}, u32[]{:S(2)}, u32[]{:S(2)}) %all-to-all-start) | async-done | bytes 852000 | tf_op jit(solution)/shard_map/all_to_all | solution.py:510
  31.8 19.3 %shard_map.75 = f32[4,2048]{1,0:T(4,128)} custom-call(s32[16,16]{1,0:T(8,128)} %refs_0_.3, s32[8,16]{1,0:T(8,128)} %bitcast.6, f32[32,13,4,128]{3,2,1,0:T(4,128)} %all-to-all-done.refs_2_, f32[4,2048]{1,0:T(4,128)} %refs_3_.5, bf16[16,128,96]{2,1,0:T(8,128)(2,1)} %get-tuple-element.8.refs_4_, f32[16,3,128,128]{3,2,1,0:T(8,128)} %get-tuple-element.9.refs_5_, ...), custom_call_target="tpu_custom_call" | custom-call | tf_op jit(solution)/shard_map/pallas_call | solution.py:532
Async XLA Ops:
  2.3 29.4 %all-to-all-start = ((f32[32,13,4,128]{3,2,1,0:T(4,128)}), f32[32,13,4,128]{3,2,1,0:T(4,128)}, u32[]{:S(2)}, u32[]{:S(2)}) async-start(f32[32,13,4,128]{3,2,1,0:T(4,128)} %shard_map.73), calls=%async_computation | async-start | bytes 1703936 | tf_op jit(solution)/shard_map/all_to_all | solution.py:510
